TPU v7x, 32 devices: a whole 2x2x4 slice. The times are simulated.
32 devices in a mesh: groups: 2 (over x), ctx: 8 (over z, y), heads: 2 (over core).
Axes of the slice: x: 2, y: 2, z: 4, core: 2. Of those that a mesh axis runs over, the one named last changes fastest.
Arguments:
- activations: bfloat16 [8192, 4096], P(('groups', 'ctx')), parts along dimension 0, may hold values from -6 to 6
- queries: bfloat16 [8192, 2048], P(('groups', 'ctx'), 'heads'), parts along dimension 0, may hold values from -6 to 6
- key_rows: bfloat16 [8192, 2048], P(('groups', 'ctx'), 'heads'), parts along dimension 0, may hold values from -6 to 6
- value_rows: bfloat16 [8192, 2048], P(('groups', 'ctx'), 'heads'), parts along dimension 0, may hold values from -6 to 6
- out_grad: bfloat16 [8192, 2048], P(('groups', 'ctx'), 'heads'), parts along dimension 0, may hold values from -6 to 6
- norm_gain: float32 [2048], P('heads'), may hold values from 0.1 to 1.9
Outputs:
- query_grad: bfloat16 [8192, 2048], P(('groups', 'ctx'), 'heads'), parts along dimension 0
- key_grad: bfloat16 [8192, 2048], P(('groups', 'ctx'), 'heads'), parts along dimension 0
- weight_grad: float32 [8192, 2048], P(('groups', 'ctx'), 'heads'), parts along dimension 0
There are 2 independent parts, one for each index of `groups`. A program takes and returns all parts, laid end to end along the dimension named above; an argument that names none is the same for every part. Nothing has to cross between parts.
All inputs are finite; a program needn't handle non-finite values.
Results may differ from a plain program's by a relative error of at most 0.015.
Values may be sent and summed in bfloat16 or wider, within the bound.
A program may use at most 128 MiB of HBM per device.

v0:
```python
import jax
import jax.numpy as jnp
from jax import lax
from jax.sharding import PartitionSpec as P

HEAD_DIM = 128


epsilon = 1e-06


def entering(x, axis, combine, identity):
    length, index = (lax.axis_size(axis), lax.axis_index(axis))
    everything = lax.all_gather(x.astype(jnp.bfloat16), axis)
    start = jnp.broadcast_to(jnp.asarray(identity, x.dtype), x.shape)

    def hop(k, before):
        at = length - 1 - k
        reached = at > index
        new = combine(before, everything[at].astype(x.dtype))
        return jnp.where(reached, new, before)

    return lax.fori_loop(0, length, hop, start)


def split_state(state):
    high = state.astype(jnp.bfloat16)
    back = lax.optimization_barrier(high).astype(jnp.float32)
    low = (state - back).astype(jnp.bfloat16)
    return (high, low)


def masked_product(left_side, right_side, causal):
    raw = jnp.einsum("thc,shc->hts", left_side, right_side, preferred_element_type=jnp.float32)
    return jnp.where(causal[None], raw, 0.0).astype(jnp.bfloat16)


def add_states(earlier, later):
    return earlier + later


def per_device(activations, queries, key_rows, value_rows, out_grad, norm_gain):
    length = queries.shape[0]
    heads_here = queries.shape[1] // HEAD_DIM
    shape_three = (length, heads_here, HEAD_DIM)
    query_heads = queries.reshape(shape_three)
    key_heads = key_rows.reshape(shape_three)
    value_heads = value_rows.reshape(shape_three)
    grad_heads = out_grad.reshape(shape_three)
    gain_heads = norm_gain.reshape(heads_here, HEAD_DIM)
    causal = jnp.arange(length)[:, None] >= jnp.arange(length)[None, :]
    kv_local = jnp.einsum(
        "thc,thd->hcd", key_heads, value_heads, preferred_element_type=jnp.float32
    )
    zero_state = jnp.zeros_like(kv_local)
    my_index = lax.axis_index("ctx")
    pieces = lax.all_gather(kv_local[None].astype(jnp.bfloat16), "ctx", axis=0, tiled=True).astype(
        jnp.float32
    )
    positions = jnp.arange(pieces.shape[0])
    weights = (positions < my_index).astype(jnp.float32)
    state_in = zero_state + jnp.sum(pieces * weights[:, None, None, None], axis=0)
    state_high, state_low = split_state(state_in)
    scores = masked_product(query_heads, key_heads, causal)
    attended = jnp.einsum("hts,shd->thd", scores, value_heads, preferred_element_type=jnp.float32)
    attended = attended + jnp.einsum(
        "thc,hcd->thd", query_heads, state_high, preferred_element_type=jnp.float32
    )
    attended = attended + jnp.einsum(
        "thc,hcd->thd", query_heads, state_low, preferred_element_type=jnp.float32
    )
    inv_rms = lax.rsqrt(jnp.mean(attended * attended, axis=-1, keepdims=True) + epsilon)
    normed = attended * inv_rms
    upstream = grad_heads.astype(jnp.float32) * gain_heads[None]
    delta = inv_rms * (upstream - normed * jnp.mean(upstream * normed, axis=-1, keepdims=True))
    delta = delta.astype(jnp.bfloat16)
    grad_local = jnp.einsum("thc,thd->hcd", query_heads, delta, preferred_element_type=jnp.float32)
    grad_in = entering(grad_local, "ctx", add_states, zero_state)
    grad_high, grad_low = split_state(grad_in)
    back_scores = masked_product(delta, value_heads, causal)
    query_grad = jnp.einsum(
        "hts,shc->thc", back_scores, key_heads, preferred_element_type=jnp.float32
    )
    query_grad = query_grad + jnp.einsum(
        "thd,hcd->thc", delta, state_high, preferred_element_type=jnp.float32
    )
    query_grad = query_grad + jnp.einsum(
        "thd,hcd->thc", delta, state_low, preferred_element_type=jnp.float32
    )
    key_grad = jnp.einsum(
        "hts,thc->shc", back_scores, query_heads, preferred_element_type=jnp.float32
    )
    key_grad = key_grad + jnp.einsum(
        "shd,hcd->shc", value_heads, grad_high, preferred_element_type=jnp.float32
    )
    key_grad = key_grad + jnp.einsum(
        "shd,hcd->shc", value_heads, grad_low, preferred_element_type=jnp.float32
    )
    value_grad = jnp.einsum("hts,thd->shd", scores, delta, preferred_element_type=jnp.float32)
    value_grad = value_grad + jnp.einsum(
        "shc,hcd->shd", key_heads, grad_high, preferred_element_type=jnp.float32
    )
    value_grad = value_grad + jnp.einsum(
        "shc,hcd->shd", key_heads, grad_low, preferred_element_type=jnp.float32
    )
    flat_shape = (length, heads_here * HEAD_DIM)
    value_flat = value_grad.astype(jnp.bfloat16).reshape(flat_shape)
    weight_grad = lax.psum_scatter(
        jnp.einsum("tr,tc->rc", activations, value_flat, preferred_element_type=jnp.float32).astype(
            jnp.bfloat16
        ),
        "ctx",
        scatter_dimension=0,
        tiled=True,
    ).astype(jnp.float32)
    return (
        query_grad.astype(jnp.bfloat16).reshape(flat_shape),
        key_grad.astype(jnp.bfloat16).reshape(flat_shape),
        weight_grad,
    )


def solution(mesh):
    placed = (
        P(("groups", "ctx"), None),
        P(("groups", "ctx"), "heads"),
        P(("groups", "ctx"), "heads"),
        P(("groups", "ctx"), "heads"),
        P(("groups", "ctx"), "heads"),
        P("heads"),
    )
    return jax.shard_map(
        per_device,
        mesh=mesh,
        in_specs=placed,
        out_specs=(
            P(("groups", "ctx"), "heads"),
            P(("groups", "ctx"), "heads"),
            P(("groups", "ctx"), "heads"),
        ),
        check_vma=False,
    )
```

profile of v0, /device:TPU:0, one launch (start us, length us, event | category | flops | bytes accessed | tf_op | source)
XLA Modules:
  0.0 298.8 jit_solution(4504855991643453436)
XLA Ops:
  7.2 2.6 copy.73
  9.8 1.6 copy.39
  11.5 1.1 convolution_convert_fusion.1
  12.7 1.5 copy.45
  14.4 2.6 select_convert_fusion.1
  17.0 1.9 copy-done.1
  19.0 2.8 fusion.4
  21.8 43.0 %all-gather.5.cloned.1.call-done = bf16[64,128,128]{2,1,0:T(8,128)(2,1)} async-done(((bf16[8,128,128]{2,1,0:T(8,128)(2,1)}), bf16[64,128,128]{2,1,0:T(8,128)(2,1)}) %all-gather.5.cloned.1.call-update) | async-done | bytes 2097168 | tf_op jit(solution)/shard_map/all_gather | solution.py:57
  64.8 2.1 fusion
  73.2 4.5 %fusion.37 = f32[8,128,512]{2,1,0:T(8,128)} fusion(bf16[512,8,128]{0,2,1:T(8,128)(2,1)} %copy-done.4, bf16[8,512,512]{2,1,0:T(8,128)(2,1)} %copy-done.1), kind=kOutput, calls=%fused_computation.60 | convolution fusion | flops 536870912 | bytes 7340032 | tf_op jit(solution)/shard_map/hts,thd->shd/dot_general | solution.py:99
  77.8 43.1 %all-gather.7.cloned.1.call-done = bf16[64,128,128]{2,1,0:T(8,128)(2,1)} async-done(((bf16[8,128,128]{2,1,0:T(8,128)(2,1)}), bf16[64,128,128]{2,1,0:T(8,128)(2,1)}) %all-gather.7.cloned.1.call-update) | async-done | bytes 2097168 | tf_op jit(solution)/shard_map/all_gather | solution.py:14
  120.9 10.2 %while.16 = (s32[]{:T(128)}, f32[8,128,128]{2,1,0:T(8,128)S(1)}, s32[]{:T(128)}, bf16[8,8,128,128]{3,2,1,0:T(8,128)(2,1)}, s32[]{:T(128)}, /*index=5*/s32[]{:T(128)}, s32[]{:T(128)}, s32[]{:T(128)}) while((s32[]{:T(128)}, f32[8,128,128]{2,1,0:T(8,128)S(1)}, s32[]{:T(128)}, bf16[8,8,128,128]{3,2,1,0:T(8,128)(2,1)}, s32[]{:T(128)}, ...), condition=%wide.region_4.5_spmd.clone, body=%wide.region_3.4_spmd.clone.sunk | while | flops 524296 | bytes 1310875 | solution.py:23
  120.9 1.3 add_select_fusion.2
  122.3 1.2 add_select_fusion.2
  123.5 1.2 add_select_fusion.2
  124.8 1.2 add_select_fusion.2
  126.1 1.2 add_select_fusion.2
  127.3 1.2 add_select_fusion.2
  128.6 1.2 add_select_fusion.2
  129.8 1.2 add_select_fusion.2
  131.7 1.0 copy-done.11
  133.3 1.5 copy-done.20
  134.9 6.8 %convert_bitcast_fusion = bf16[4096,1024]{0,1:T(8,128)(2,1)} fusion(bf16[512,1024]{0,1:T(8,128)(2,1)S(1)} %bitcast.146, bf16[512,4096]{1,0:T(8,128)(2,1)S(1)} %copy-done.20), kind=kOutput, calls=%fused_computation.1 | convolution fusion | flops 4299161600 | bytes 13631488 | tf_op jit(solution)/shard_map/tr,tc->rc/dot_general | solution.py:109
  141.7 1.2 copy-done.5
  144.1 1.4 select_convert_fusion
  145.6 1.5 fusion.35
  147.9 1.5 fusion.2
  149.3 2.4 copy.60
  152.6 1.3 copy-done.3
  154.7 1.3 copy.61
  156.1 133.7 %reduce-scatter.2.cloned.1.call-done = bf16[512,1024]{0,1:T(8,128)(2,1)} async-done(((bf16[4096,1024]{0,1:T(8,128)(2,1)}), bf16[512,1024]{0,1:T(8,128)(2,1)}) %reduce-scatter.2.cloned.1.call-update) | async-done | bytes 1048592 | tf_op jit(solution)/shard_map/reduce_scatter | solution.py:108
  289.7 2.6 copy.62
  (62 shorter events, 11.4 us)
Async XLA Ops:
  7.2 7.2 %copy-start = (bf16[512,1024]{1,0:T(8,128)(2,1)S(1)}, bf16[512,1024]{1,0:T(8,128)(2,1)}, u32[]{:S(2)}) copy-start(bf16[512,1024]{1,0:T(8,128)(2,1)} %param.9) | copy-start | bytes 3145732
  7.2 57.6 %all-gather.5.cloned.1.call-start = ((), (), s32[]{:S(2)}) async-start(), calls=%async_computation.2 | async-start | bytes 2359296 | tf_op jit(solution)/shard_map/all_gather | solution.py:57
  7.2 4.3 %copy-start.7 = (bf16[512,1024]{1,0:T(8,128)(2,1)S(1)}, bf16[512,1024]{1,0:T(8,128)(2,1)}, u32[]{:S(2)}) copy-start(bf16[512,1024]{1,0:T(8,128)(2,1)} %param.11) | copy-start | bytes 3145732
  11.5 1.2 copy-start.15
  12.7 108.2 %all-gather.7.cloned.1.call-start = ((), (), s32[]{:S(2)}) async-start(), calls=%async_computation.3 | async-start | bytes 2359296 | tf_op jit(solution)/shard_map/all_gather | solution.py:14
  14.4 2.7 copy-start.17
  14.4 4.6 %copy-start.8 = (bf16[512,1024]{1,0:T(8,128)(2,1)S(1)}, bf16[512,1024]{1,0:T(8,128)(2,1)}, u32[]{:S(2)}) copy-start(bf16[512,1024]{1,0:T(8,128)(2,1)} %param.11) | copy-start | bytes 3145732
  17.0 1.9 copy-start.1
  67.0 0.8 copy-start.12
  67.0 1.8 copy-start.14
  68.8 0.8 copy-start.19
  70.6 1.0 copy-start.4
  73.0 216.8 %reduce-scatter.2.cloned.1.call-start = ((), (), s32[]{:S(2)}) async-start(), calls=%async_computation.1 | async-start | bytes 9437184 | tf_op jit(solution)/shard_map/reduce_scatter | solution.py:108
  120.9 10.2 %copy-start.6 = (bf16[512,1024]{1,0:T(8,128)(2,1)S(1)}, bf16[512,1024]{1,0:T(8,128)(2,1)}, u32[]{:S(2)}) copy-start(bf16[512,1024]{1,0:T(8,128)(2,1)} %param.10) | copy-start | bytes 3145732
  131.1 1.6 copy-start.11
  132.7 2.2 copy-start.20
  141.7 1.2 copy-start.5
  142.9 1.2 copy-start.9
  142.9 1.3 copy-start.18
  144.1 1.5 copy-start.16
  145.6 2.3 copy-start.2
  145.6 2.3 copy-start.13
  149.3 2.4 copy-start.10
  151.7 2.2 copy-start.3
Sparse Core Ops, SparseCore 0:
  12.8 51.9 all-gather.4
  73.1 47.7 all-gather.6
  141.8 147.8 reduce-scatter.1
where the time goes:
time: 300 us; the launch traced here: 299 us
  waiting for transfers between devices  220 us (73%)
  matrix products  27.3 us (9%)
  local copies, waits for them, and re-layouts  23.7 us (8%)
  between operations  14.1 us (5%)
  other arithmetic  13.4 us (4%)
    reduce_scatter x1, waiting for transfers between devices, per_device(): lax.psum_scatter(jnp.einsum('tr,tc->rc', activations, value_flat, preferr...  134 us
    all_gather x1, waiting for transfers between devices, entering(): everything = lax.all_gather(x.astype(jnp.bfloat16), axis)  43.1 us
    all_gather x1, waiting for transfers between devices, per_device(): lax.all_gather(kv_local[None].astype(jnp.bfloat16), 'ctx', axis=0, tiled=...  43 us
    unnamed x46, local copies, waits for them, and re-layouts  19.7 us
    select_n x8, other arithmetic, hop(): return jnp.where(reached, new, before)  9.96 us
    dot_general x1, matrix products, per_device(): jnp.einsum('tr,tc->rc', activations, value_flat, preferred_element_type=j...  6.77 us
  transfers between devices with their start and end apart: 3, of which 3 were waited for; matrix products, arithmetic and copies ran while one was open for 7% of the time, Pallas kernels for 0%

commit v1 on v0

v1 whole, which is shorter than its diff:
```python
import functools

import jax
import jax.numpy as jnp
from jax import lax
from jax.experimental import pallas as pl
from jax.experimental.pallas import tpu as pltpu
from jax.sharding import PartitionSpec as P

HEAD_DIM = 128
EPSILON = 1e-06
MESH = pl.DeviceIdType.MESH
F32 = jnp.float32
BF16 = jnp.bfloat16


def dot(a, b, ca, cb):
    return lax.dot_general(a, b, (((ca,), (cb,)), ((), ())), preferred_element_type=F32)


def split_state(state):
    high = state.astype(BF16)
    return high, (state - high.astype(F32)).astype(BF16)


def kernel(
    n, chunks,
    act, q_in, k_in, v_in, g_in, gain,
    qg_out, kg_out, w_out,
    q, k, v, g, acts, vals, scores, delta, att, vg_acc, kg_acc, qg, kg, wg,
    kv_mine, kv_pair, kv_send, kv_recv, st_high, st_low,
    gl_mine, gl_pair, gl_send, gl_recv,
    right_out, right_in, left_out, left_in,
    in_sem, own_sem, out_sem,
    act_ssem, act_rsem, sib_sem,
    kvp_s, kvp_r, kvc_s, kvc_r,
    glp_s, glp_r, glc_s, glc_r,
    val_s, val_r,
    rt_s, rt_r, lt_s, lt_r,
):
    tok, width = q.shape
    heads = width // HEAD_DIM
    per = heads // chunks
    span = per * HEAD_DIM
    rows = n // 2
    own = act.shape[1] // n
    me = lax.axis_index("ctx")
    core = lax.axis_index("heads")
    z = me // 2
    y = me % 2
    pair = me + 1 - 2 * y
    half = rows // 2

    def load(i, src, dst):
        return pltpu.make_async_copy(src, dst, in_sem.at[i])

    loads = [load(0, k_in, k), load(1, v_in, v), load(2, q_in, q), load(3, g_in, g)]
    for c in loads:
        c.start()

    def own_act(b):
        src = pl.multiple_of((2 * b + y) * own, 128)
        return pltpu.make_async_copy(
            act.at[:, pl.ds(src, own)],
            acts.at[pl.ds(0, tok), pl.ds(pl.multiple_of(b * own, 128), own)],
            own_sem.at[b],
        )

    def send_act(j):
        b = core * half + j
        src = pl.multiple_of((2 * b + 1 - y) * own, 128)
        return pltpu.make_async_remote_copy(
            src_ref=act.at[:, pl.ds(src, own)],
            dst_ref=acts.at[pl.ds(tok, tok), pl.ds(pl.multiple_of(b * own, 128), own)],
            send_sem=act_ssem.at[j], recv_sem=act_rsem.at[j],
            device_id={"ctx": pair}, device_id_type=MESH,
        )

    def share_act():
        at = acts.at[pl.ds(tok, tok), pl.ds(pl.multiple_of(core * half * own, 128), half * own)]
        return pltpu.make_async_remote_copy(
            src_ref=at, dst_ref=at, send_sem=sib_sem.at[0], recv_sem=sib_sem.at[1],
            device_id={"heads": 1 - core}, device_id_type=MESH,
        )

    def heads_copy(src, dst, ssem, rsem, to, c):
        at = pl.ds(c * per, per)
        return pltpu.make_async_remote_copy(
            src_ref=src.at[at], dst_ref=dst.at[at],
            send_sem=ssem.at[c], recv_sem=rsem.at[c],
            device_id={"ctx": to}, device_id_type=MESH,
        )

    def send_val(c):
        cols = pl.ds(pl.multiple_of(c * span, 128), span)
        return pltpu.make_async_remote_copy(
            src_ref=vals.at[pl.ds(0, tok), cols], dst_ref=vals.at[pl.ds(tok, tok), cols],
            send_sem=val_s.at[c], recv_sem=val_r.at[c],
            device_id={"ctx": pair}, device_id_type=MESH,
        )

    def block_copy(src, dst, ssem, rsem, to, b, c):
        return pltpu.make_async_remote_copy(
            src_ref=src.at[b, c], dst_ref=dst.at[b, c],
            send_sem=ssem.at[b, c], recv_sem=rsem.at[b, c],
            device_id={"ctx": to}, device_id_type=MESH,
        )

    def right_copy(b, c):
        return block_copy(right_out, right_in, rt_s, rt_r, lax.rem(me + 2, n), b, c)

    def left_copy(b, c):
        return block_copy(left_out, left_in, lt_s, lt_r, lax.rem(me + n - 2, n), b, c)

    def kv_pair_copy(c):
        return heads_copy(kv_mine, kv_pair, kvp_s, kvp_r, pair, c)

    def kv_chain(c):
        return heads_copy(kv_send, kv_recv, kvc_s, kvc_r, lax.rem(me + 2, n), c)

    def gl_pair_copy(c):
        return heads_copy(gl_mine, gl_pair, glp_s, glp_r, pair, c)

    def gl_chain(c):
        return heads_copy(gl_send, gl_recv, glc_s, glc_r, lax.rem(me + n - 2, n), c)

    def loop(count, body):
        def step(i, carry):
            body(i)
            return carry
        lax.fori_loop(0, count, step, 0)

    def each_head(c, body):
        for i in range(per):
            h = c * per + i
            body(h, pl.ds(pl.multiple_of(h * HEAD_DIM, 128), HEAD_DIM))

    has_left = z > 0
    has_right = z < rows - 1

    barrier = pltpu.get_barrier_semaphore()
    pl.semaphore_signal(barrier, inc=1, device_id={"ctx": pair}, device_id_type=MESH)
    pl.semaphore_signal(barrier, inc=1, device_id={"heads": 1 - core}, device_id_type=MESH)

    @pl.when(has_left)
    def _():
        pl.semaphore_signal(barrier, inc=1, device_id={"ctx": me - 2}, device_id_type=MESH)

    @pl.when(has_right)
    def _():
        pl.semaphore_signal(barrier, inc=1, device_id={"ctx": me + 2}, device_id_type=MESH)

    ends = has_left.astype(jnp.int32) + has_right.astype(jnp.int32)
    pl.semaphore_wait(barrier, 2 + ends)

    loads[0].wait()
    loads[1].wait()

    def summaries(c):
        def one(h, cols):
            kv_mine[h] = dot(k[:, cols], v[:, cols], 0, 0).astype(BF16)
        each_head(c, one)
        kv_pair_copy(c).start()
    loop(chunks, summaries)

    loop(half, lambda j: send_act(j).start())
    loop(rows, lambda b: own_act(b).start())

    @pl.when(jnp.logical_not(has_left))
    def _():
        kv_recv[...] = jnp.zeros_like(kv_recv)

    @pl.when(jnp.logical_not(has_right))
    def _():
        gl_recv[...] = jnp.zeros_like(gl_recv)

    loads[2].wait()
    loads[3].wait()

    def causal(raw):
        t = lax.broadcasted_iota(jnp.int32, raw.shape, 0)
        s = lax.broadcasted_iota(jnp.int32, raw.shape, 1)
        return jnp.where(s <= t, raw, 0.0).astype(BF16)

    def score(c):
        def one(h, cols):
            s = causal(dot(q[:, cols], k[:, cols], 1, 1))
            scores[h] = s
            att[:, cols] = dot(s, v[:, cols], 1, 0)
        each_head(c, one)
    loop(chunks, score)

    def forward(c):
        kv_pair_copy(c).wait()

        @pl.when(has_left)
        def _():
            kv_chain(c).wait_recv()

        def state(h, cols):
            carry = kv_recv[h].astype(F32)
            other = kv_pair[h].astype(F32)
            kv_send[h] = (carry + other + kv_mine[h].astype(F32)).astype(BF16)
            high, low = split_state(carry + jnp.where(y == 1, other, 0.0))
            st_high[h] = high
            st_low[h] = low
        each_head(c, state)

        @pl.when(has_right)
        def _():
            kv_chain(c).start()

        def one(h, cols):
            qh = q[:, cols]
            a = att[:, cols] + dot(qh, st_high[h], 1, 0) + dot(qh, st_low[h], 1, 0)
            inv = lax.rsqrt(jnp.mean(a * a, axis=-1, keepdims=True) + EPSILON)
            normed = a * inv
            up = g[:, cols].astype(F32) * gain[:, cols]
            d = inv * (up - normed * jnp.mean(up * normed, axis=-1, keepdims=True))
            d = d.astype(BF16)
            delta[:, cols] = d
            gl_mine[h] = dot(qh, d, 0, 0).astype(BF16)
        each_head(c, one)
        gl_pair_copy(c).start()
    loop(chunks, forward)

    loop(half, lambda j: send_act(j).wait())
    share_act().start()

    def inside(c):
        def one(h, cols):
            d = delta[:, cols]
            back = causal(dot(d, v[:, cols], 1, 1))
            x = dot(back, k[:, cols], 1, 0)
            x = x + dot(d, st_high[h], 1, 1) + dot(d, st_low[h], 1, 1)
            qg[:, cols] = x.astype(BF16)
            kg_acc[:, cols] = dot(back, q[:, cols], 0, 0)
            vg_acc[:, cols] = dot(scores[h], d, 0, 0)
        each_head(c, one)
    loop(chunks, inside)
    qg_copy = pltpu.make_async_copy(qg, qg_out, out_sem.at[0])
    qg_copy.start()

    def backward(c):
        gl_pair_copy(c).wait()

        @pl.when(has_right)
        def _():
            gl_chain(c).wait_recv()

        def one(h, cols):
            carry = gl_recv[h].astype(F32)
            other = gl_pair[h].astype(F32)
            gl_send[h] = (carry + other + gl_mine[h].astype(F32)).astype(BF16)
        each_head(c, one)

        @pl.when(has_left)
        def _():
            gl_chain(c).start()

        def two(h, cols):
            carry = gl_recv[h].astype(F32)
            other = gl_pair[h].astype(F32)
            high, low = split_state(carry + jnp.where(y == 0, other, 0.0))
            kh = k[:, cols]
            x = vg_acc[:, cols] + dot(kh, high, 1, 0) + dot(kh, low, 1, 0)
            vals[0:tok, cols] = x.astype(BF16)
            vh = v[:, cols]
            x = kg_acc[:, cols] + dot(vh, high, 1, 1) + dot(vh, low, 1, 1)
            kg[:, cols] = x.astype(BF16)
        each_head(c, two)
        send_val(c).start()
    loop(chunks, backward)
    kg_copy = pltpu.make_async_copy(kg, kg_out, out_sem.at[1])
    kg_copy.start()

    loop(rows, lambda b: own_act(b).wait())
    share_act().wait()

    def term(b, c):
        a = acts[:, pl.ds(pl.multiple_of(b * own, 128), own)]
        x = vals[:, pl.ds(pl.multiple_of(c * span, 128), span)]
        return dot(a, x, 0, 0)

    def products(c):
        send_val(c).wait()

        def step(j):
            r = rows - 1 - j

            @pl.when(r > z)
            def _():
                x = term(r, c)

                @pl.when(has_left)
                def _():
                    right_copy(r, c).wait_recv()
                    right_out[r, c] = (x + right_in[r, c].astype(F32)).astype(BF16)

                @pl.when(jnp.logical_not(has_left))
                def _():
                    right_out[r, c] = x.astype(BF16)
                right_copy(r, c).start()

            @pl.when(j < z)
            def _():
                x = term(j, c)

                @pl.when(has_right)
                def _():
                    left_copy(j, c).wait_recv()
                    left_out[j, c] = (x + left_in[j, c].astype(F32)).astype(BF16)

                @pl.when(jnp.logical_not(has_right))
                def _():
                    left_out[j, c] = x.astype(BF16)
                left_copy(j, c).start()
        loop(rows, step)
        wg[c] = term(z, c)
    loop(chunks, products)

    def w_copy(c):
        return pltpu.make_async_copy(
            wg.at[c], w_out.at[:, pl.ds(pl.multiple_of(c * span, 128), span)], out_sem.at[2 + c]
        )

    def finish(c):
        @pl.when(has_left)
        def _():
            right_copy(z, c).wait_recv()
            wg[c] = wg[c] + right_in[z, c].astype(F32)

        @pl.when(has_right)
        def _():
            left_copy(z, c).wait_recv()
            wg[c] = wg[c] + left_in[z, c].astype(F32)
        w_copy(c).start()
    loop(chunks, finish)

    def drain(c):
        @pl.when(has_right)
        def _():
            kv_chain(c).wait_send()

        @pl.when(has_left)
        def _():
            gl_chain(c).wait_send()

        def step(b):
            @pl.when(b > z)
            def _():
                right_copy(b, c).wait_send()

            @pl.when(b < z)
            def _():
                left_copy(b, c).wait_send()
        loop(rows, step)
        w_copy(c).wait()
    loop(chunks, drain)
    qg_copy.wait()
    kg_copy.wait()


def per_device(n, activations, queries, key_rows, value_rows, out_grad, norm_gain):
    tok, width = queries.shape
    deep = activations.shape[1]
    own = deep // n
    rows = n // 2
    heads = width // HEAD_DIM
    chunks = 4
    span = width // chunks
    states = pltpu.VMEM((heads, HEAD_DIM, HEAD_DIM), BF16)
    blocks = pltpu.VMEM((rows, chunks, own, span), BF16)
    slab = pltpu.VMEM((tok, width), BF16)
    wide = pltpu.VMEM((tok, width), F32)
    dma = pltpu.SemaphoreType.DMA
    hbm = pl.BlockSpec(memory_space=pl.ANY)
    flops = 2 * tok * deep * width + 2 * heads * tok * HEAD_DIM * (6 * tok + 10 * HEAD_DIM)
    return pl.pallas_call(
        functools.partial(kernel, n, chunks),
        out_shape=(
            jax.ShapeDtypeStruct((tok, width), BF16),
            jax.ShapeDtypeStruct((tok, width), BF16),
            jax.ShapeDtypeStruct((own, width), F32),
        ),
        in_specs=[hbm] * 5 + [pl.BlockSpec(memory_space=pltpu.VMEM)],
        out_specs=(hbm, hbm, hbm),
        scratch_shapes=[
            slab, slab, slab, slab,
            pltpu.VMEM((2 * tok, rows * own), BF16),
            pltpu.VMEM((2 * tok, width), BF16),
            pltpu.VMEM((heads, tok, tok), BF16),
            slab, wide, wide, wide, slab, slab,
            pltpu.VMEM((chunks, own, span), F32),
        ] + [states] * 10 + [blocks] * 4 + [
            dma((4,)), dma((rows,)), dma((2 + chunks,)),
            dma((rows // 2,)), dma((rows // 2,)), dma((2,)),
        ] + [dma((chunks,))] * 10 + [dma((rows, chunks))] * 4,
        compiler_params=pltpu.CompilerParams(
            collective_id=0, has_side_effects=True, vmem_limit_bytes=60 * 1024 * 1024
        ),
        cost_estimate=pl.CostEstimate(flops=flops, bytes_accessed=17 * 2**20, transcendentals=0),
    )(activations, queries, key_rows, value_rows, out_grad, norm_gain.reshape(1, width))


def solution(mesh):
    rows = P(("groups", "ctx"), None)
    split = P(("groups", "ctx"), "heads")
    return jax.shard_map(
        functools.partial(per_device, mesh.shape["ctx"]),
        mesh=mesh,
        in_specs=(rows, split, split, split, split, P("heads")),
        out_specs=(split, split, split),
        check_vma=False,
    )
```

time: 300 us -> 160 us (0.53)
  waiting for transfers between devices: 220 us -> 0 us
  Pallas kernels: 0 us -> 155 us
  matrix products: 27.3 us -> 0 us
  local copies, waits for them, and re-layouts: 23.7 us -> 4.71 us
  between operations: 14.1 us -> 0.66 us
  other arithmetic: 13.4 us -> 0 us
    pallas_call x0 -> x1, Pallas kernels: none -> 155 us  [per_device(): pl.pallas_call(functools.partial(kernel, n, chunks), out_shape=(jax.Shape...]
    reduce_scatter x1 -> x0, waiting for transfers between devices: 134 us -> none  [per_device(): lax.psum_scatter(jnp.einsum('tr,tc->rc', activations, value_flat, preferr...]
    all_gather x2 -> x0, waiting for transfers between devices: 86.2 us -> none  [the longest x1 43.1 us: entering(): everything = lax.all_gather(x.astype(jnp.bfloat16), axis)]
    dot_general x17 -> x0, matrix products: 27.3 us -> none  [the longest x1 6.77 us: per_device(): jnp.einsum('tr,tc->rc', activations, value_flat, preferred_element_type=j...]
    unnamed x46 -> x7, local copies, waits for them, and re-layouts: 19.7 us -> 4.71 us
    select_n x8 -> x0, other arithmetic: 9.96 us -> none  [hop(): return jnp.where(reached, new, before)]
  transfers between devices with their start and end apart: 3 -> 0, of which waited for: 3 -> 0; matrix products, arithmetic and copies ran while one was open for 7% -> 0% of each run, Pallas kernels for 0% -> 0%
where the time goes in v1:
time: 160 us
  Pallas kernels  155 us (97%)
  local copies, waits for them, and re-layouts  4.71 us (3%)
    pallas_call x1, Pallas kernels, per_device(): pl.pallas_call(functools.partial(kernel, n, chunks), out_shape=(jax.Shape...  155 us
    unnamed x7, local copies, waits for them, and re-layouts  4.71 us

profile of v1, /device:TPU:0, one launch (start us, length us, event | category | flops | bytes accessed | tf_op | source)
XLA Modules:
  0.0 160.0 jit_solution(16649583800796879566)
XLA Ops:
  0.6 154.6 %shard_map.85 = (bf16[512,1024]{1,0:T(8,128)(2,1)}, bf16[512,1024]{1,0:T(8,128)(2,1)}, f32[512,1024]{1,0:T(8,128)}) custom-call(bf16[512,4096]{1,0:T(8,128)(2,1)} %act.1, bf16[512,1024]{1,0:T(8,128)(2,1)} %q_in.1, bf16[512,1024]{1,0:T(8,128)(2,1)} %k_in.1, bf16[512,1024]{1,0:T(8,128)(2,1)} %v_in.1, bf16[512,1024]{1,0:T(8,128)(2,1)} %g_in.1, f32[1,1024]{1,0:T(1,128)} %bitcast.1), custom_call_target="tpu_custom_call" | custom-call | flops 8858370048 | bytes 17825792 | tf_op jit(solution)/shard_map/pallas_call | solution.py:379
  155.3 0.0 copy-start.1
  155.3 0.0 copy-start
  155.3 2.4 %copy.12 = bf16[512,1024]{1,0:T(8,128)(2,1)} copy(bf16[512,1024]{1,0:T(8,128)(2,1)} %get-tuple-element.6) | data formatting | bytes 2097152
  157.7 0.0 copy-done.1
  157.7 1.0 copy.13
  158.7 0.0 copy-done
  158.7 1.3 copy.14
Async XLA Ops:
  155.3 2.4 %copy-start.1 = (bf16[512,1024]{1,0:T(8,128)(2,1)S(1)}, bf16[512,1024]{1,0:T(8,128)(2,1)}, u32[]{:S(2)}) copy-start(bf16[512,1024]{1,0:T(8,128)(2,1)} %get-tuple-element.7) | copy-start | bytes 3145732
  155.3 3.4 %copy-start = (f32[512,1024]{1,0:T(8,128)S(1)}, f32[512,1024]{1,0:T(8,128)}, u32[]{:S(2)}) copy-start(f32[512,1024]{1,0:T(8,128)} %get-tuple-element.8) | copy-start | bytes 6291460

commit v2 on v1

--- a/solution.py
+++ b/solution.py
@@ -30,13 +30,14 @@
     q, k, v, g, acts, vals, scores, delta, att, vg_acc, kg_acc, qg, kg, wg,
     kv_mine, kv_pair, kv_send, kv_recv, st_high, st_low,
     gl_mine, gl_pair, gl_send, gl_recv,
-    right_out, right_in, left_out, left_in,
+    right_out, right_in, left_out, left_in, acts_edge, vals_edge,
     in_sem, own_sem, out_sem,
     act_ssem, act_rsem, sib_sem,
     kvp_s, kvp_r, kvc_s, kvc_r,
     glp_s, glp_r, glc_s, glc_r,
     val_s, val_r,
     rt_s, rt_r, lt_s, lt_r,
+    ship_s, ship_r, relay_s, relay_r, vship_s, vship_r,
 ):
     tok, width = q.shape
     heads = width // HEAD_DIM
@@ -50,6 +51,15 @@
     y = me % 2
     pair = me + 1 - 2 * y
     half = rows // 2
+    near_left = z < half
+    near_right = z >= half
+    has_left = z > 0
+    has_right = z < rows - 1
+    middle = has_left & has_right
+    edge = jnp.logical_not(middle)
+    after_edge = z == 1
+    before_edge = z == rows - 2
+    inside_edge = after_edge | before_edge
 
     def load(i, src, dst):
         return pltpu.make_async_copy(src, dst, in_sem.at[i])
@@ -83,6 +93,36 @@
             device_id={"heads": 1 - core}, device_id_type=MESH,
         )
 
+    def edge_rows(p):
+        return pl.ds(pl.multiple_of(p * tok + core * (tok // 2), 16), tok // 2)
+
+    edge_cols = pl.ds(pl.multiple_of(jnp.where(near_left, own, 0), 128), (rows - 1) * own)
+    inner = jnp.where(near_left, lax.rem(me + 2, n), lax.rem(me + n - 2, n))
+
+    def ship(p):
+        at = edge_rows(p)
+        return pltpu.make_async_remote_copy(
+            src_ref=acts.at[at, edge_cols], dst_ref=acts_edge.at[at, edge_cols],
+            send_sem=ship_s.at[p], recv_sem=ship_r.at[p],
+            device_id={"ctx": inner}, device_id_type=MESH,
+        )
+
+    def relay(p):
+        at = acts_edge.at[edge_rows(p), edge_cols]
+        return pltpu.make_async_remote_copy(
+            src_ref=at, dst_ref=at, send_sem=relay_s.at[p], recv_sem=relay_r.at[p],
+            device_id={"heads": 1 - core}, device_id_type=MESH,
+        )
+
+    def ship_val(p, c):
+        at = pl.ds(p * tok, tok)
+        cols = pl.ds(pl.multiple_of(c * span, 128), span)
+        return pltpu.make_async_remote_copy(
+            src_ref=vals.at[at, cols], dst_ref=vals_edge.at[at, cols],
+            send_sem=vship_s.at[p, c], recv_sem=vship_r.at[p, c],
+            device_id={"ctx": inner}, device_id_type=MESH,
+        )
+
     def heads_copy(src, dst, ssem, rsem, to, c):
         at = pl.ds(c * per, per)
         return pltpu.make_async_remote_copy(
@@ -135,9 +175,6 @@
             h = c * per + i
             body(h, pl.ds(pl.multiple_of(h * HEAD_DIM, 128), HEAD_DIM))
 
-    has_left = z > 0
-    has_right = z < rows - 1
-
     barrier = pltpu.get_barrier_semaphore()
     pl.semaphore_signal(barrier, inc=1, device_id={"ctx": pair}, device_id_type=MESH)
     pl.semaphore_signal(barrier, inc=1, device_id={"heads": 1 - core}, device_id_type=MESH)
@@ -153,6 +190,11 @@
     ends = has_left.astype(jnp.int32) + has_right.astype(jnp.int32)
     pl.semaphore_wait(barrier, 2 + ends)
 
+    @pl.when(near_right)
+    def _():
+        loop(half, lambda j: send_act(j).start())
+
+    loop(rows, lambda b: own_act(b).start())
     loads[0].wait()
     loads[1].wait()
 
@@ -163,8 +205,11 @@
         kv_pair_copy(c).start()
     loop(chunks, summaries)
 
-    loop(half, lambda j: send_act(j).start())
-    loop(rows, lambda b: own_act(b).start())
+    loop(rows, lambda b: own_act(b).wait())
+
+    @pl.when(jnp.logical_not(has_right))
+    def _():
+        ship(0).start()
 
     @pl.when(jnp.logical_not(has_left))
     def _():
@@ -192,6 +237,10 @@
 
     def forward(c):
         kv_pair_copy(c).wait()
+
+        @pl.when(near_left & (c == chunks - 1))
+        def _():
+            loop(half, lambda j: send_act(j).start())
 
         @pl.when(has_left)
         def _():
@@ -224,8 +273,43 @@
         gl_pair_copy(c).start()
     loop(chunks, forward)
 
-    loop(half, lambda j: send_act(j).wait())
-    share_act().start()
+    def carry_grads(c):
+        gl_pair_copy(c).wait()
+
+        @pl.when(has_right)
+        def _():
+            gl_chain(c).wait_recv()
+
+        def one(h, cols):
+            carry = gl_recv[h].astype(F32)
+            other = gl_pair[h].astype(F32)
+            gl_send[h] = (carry + other + gl_mine[h].astype(F32)).astype(BF16)
+        each_head(c, one)
+
+        @pl.when(has_left)
+        def _():
+            gl_chain(c).start()
+
+    def gather_act():
+        loop(half, lambda j: send_act(j).wait())
+        share_act().start()
+        share_act().wait()
+
+        @pl.when(edge)
+        def _():
+            ship(1).start()
+
+    @pl.when(jnp.logical_not(has_left))
+    def _():
+        ship(0).start()
+
+    @pl.when(jnp.logical_not(has_right))
+    def _():
+        loop(chunks, carry_grads)
+
+    @pl.when(near_right)
+    def _():
+        gather_act()
 
     def inside(c):
         def one(h, cols):
@@ -238,25 +322,18 @@
             vg_acc[:, cols] = dot(scores[h], d, 0, 0)
         each_head(c, one)
     loop(chunks, inside)
+
+    @pl.when(near_left)
+    def _():
+        gather_act()
+
     qg_copy = pltpu.make_async_copy(qg, qg_out, out_sem.at[0])
     qg_copy.start()
 
     def backward(c):
-        gl_pair_copy(c).wait()
-
         @pl.when(has_right)
         def _():
-            gl_chain(c).wait_recv()
-
-        def one(h, cols):
-            carry = gl_recv[h].astype(F32)
-            other = gl_pair[h].astype(F32)
-            gl_send[h] = (carry + other + gl_mine[h].astype(F32)).astype(BF16)
-        each_head(c, one)
-
-        @pl.when(has_left)
-        def _():
-            gl_chain(c).start()
+            carry_grads(c)
 
         def two(h, cols):
             carry = gl_recv[h].astype(F32)
@@ -270,53 +347,80 @@
             kg[:, cols] = x.astype(BF16)
         each_head(c, two)
         send_val(c).start()
+
+        @pl.when(edge)
+        def _():
+            ship_val(0, c).start()
     loop(chunks, backward)
     kg_copy = pltpu.make_async_copy(kg, kg_out, out_sem.at[1])
     kg_copy.start()
 
-    loop(rows, lambda b: own_act(b).wait())
-    share_act().wait()
+    @pl.when(inside_edge)
+    def _():
+        for p in range(2):
+            ship(p).wait_recv()
+            relay(p).start()
+        for p in range(2):
+            relay(p).wait()
 
     def term(b, c):
         a = acts[:, pl.ds(pl.multiple_of(b * own, 128), own)]
         x = vals[:, pl.ds(pl.multiple_of(c * span, 128), span)]
         return dot(a, x, 0, 0)
 
+    def edge_term(b, c):
+        a = acts_edge[:, pl.ds(pl.multiple_of(b * own, 128), own)]
+        x = vals_edge[:, pl.ds(pl.multiple_of(c * span, 128), span)]
+        return dot(a, x, 0, 0)
+
     def products(c):
         send_val(c).wait()
 
+        @pl.when(edge)
+        def _():
+            ship_val(1, c).start()
+
+        @pl.when(inside_edge)
+        def _():
+            ship_val(0, c).wait_recv()
+            ship_val(1, c).wait_recv()
+
         def step(j):
             r = rows - 1 - j
 
-            @pl.when(r > z)
+            @pl.when(middle & (r > z))
             def _():
                 x = term(r, c)
 
-                @pl.when(has_left)
+                @pl.when(after_edge)
+                def _():
+                    right_out[r, c] = (x + edge_term(r, c)).astype(BF16)
+
+                @pl.when(jnp.logical_not(after_edge))
                 def _():
                     right_copy(r, c).wait_recv()
                     right_out[r, c] = (x + right_in[r, c].astype(F32)).astype(BF16)
-
-                @pl.when(jnp.logical_not(has_left))
-                def _():
-                    right_out[r, c] = x.astype(BF16)
                 right_copy(r, c).start()
 
-            @pl.when(j < z)
+            @pl.when(middle & (j < z))
             def _():
                 x = term(j, c)
 
-                @pl.when(has_right)
+                @pl.when(before_edge)
+                def _():
+                    left_out[j, c] = (x + edge_term(j, c)).astype(BF16)
+
+                @pl.when(jnp.logical_not(before_edge))
                 def _():
                     left_copy(j, c).wait_recv()
                     left_out[j, c] = (x + left_in[j, c].astype(F32)).astype(BF16)
-
-                @pl.when(jnp.logical_not(has_right))
-                def _():
-                    left_out[j, c] = x.astype(BF16)
                 left_copy(j, c).start()
         loop(rows, step)
         wg[c] = term(z, c)
+
+        @pl.when(inside_edge)
+        def _():
+            wg[c] = wg[c] + edge_term(z, c)
     loop(chunks, products)
 
     def w_copy(c):
@@ -325,12 +429,12 @@
         )
 
     def finish(c):
-        @pl.when(has_left)
+        @pl.when(z > 1)
         def _():
             right_copy(z, c).wait_recv()
             wg[c] = wg[c] + right_in[z, c].astype(F32)
 
-        @pl.when(has_right)
+        @pl.when(z < rows - 2)
         def _():
             left_copy(z, c).wait_recv()
             wg[c] = wg[c] + left_in[z, c].astype(F32)
@@ -347,16 +451,26 @@
             gl_chain(c).wait_send()
 
         def step(b):
-            @pl.when(b > z)
+            @pl.when(middle & (b > z))
             def _():
                 right_copy(b, c).wait_send()
 
-            @pl.when(b < z)
+            @pl.when(middle & (b < z))
             def _():
                 left_copy(b, c).wait_send()
         loop(rows, step)
+
+        @pl.when(edge)
+        def _():
+            ship_val(0, c).wait_send()
+            ship_val(1, c).wait_send()
         w_copy(c).wait()
     loop(chunks, drain)
+
+    @pl.when(edge)
+    def _():
+        ship(0).wait_send()
+        ship(1).wait_send()
     qg_copy.wait()
     kg_copy.wait()
 
@@ -393,9 +507,10 @@
             slab, wide, wide, wide, slab, slab,
             pltpu.VMEM((chunks, own, span), F32),
         ] + [states] * 10 + [blocks] * 4 + [
+            pltpu.VMEM((2 * tok, rows * own), BF16), pltpu.VMEM((2 * tok, width), BF16),
             dma((4,)), dma((rows,)), dma((2 + chunks,)),
             dma((rows // 2,)), dma((rows // 2,)), dma((2,)),
-        ] + [dma((chunks,))] * 10 + [dma((rows, chunks))] * 4,
+        ] + [dma((chunks,))] * 10 + [dma((rows, chunks))] * 4 + [dma((2,))] * 4 + [dma((2, chunks))] * 2,
         compiler_params=pltpu.CompilerParams(
             collective_id=0, has_side_effects=True, vmem_limit_bytes=60 * 1024 * 1024
         ),

time: 160 us -> 169 us (1.056)
  Pallas kernels: 155 us -> 164 us
    pallas_call x1, Pallas kernels: 155 us -> 164 us  [per_device(): pl.pallas_call(functools.partial(kernel, n, chunks), out_shape=(jax.Shape...]
where the time goes in v2:
time: 169 us
  Pallas kernels  164 us (97%)
  local copies, waits for them, and re-layouts  4.71 us (3%)
    pallas_call x1, Pallas kernels, per_device(): pl.pallas_call(functools.partial(kernel, n, chunks), out_shape=(jax.Shape...  164 us
    unnamed x7, local copies, waits for them, and re-layouts  4.71 us

profile of v2, /device:TPU:0, one launch (start us, length us, event | category | flops | bytes accessed | tf_op | source)
XLA Modules:
  0.0 169.1 jit_solution(16066348115827038468)
XLA Ops:
  0.6 163.7 %shard_map.85 = (bf16[512,1024]{1,0:T(8,128)(2,1)}, bf16[512,1024]{1,0:T(8,128)(2,1)}, f32[512,1024]{1,0:T(8,128)}) custom-call(bf16[512,4096]{1,0:T(8,128)(2,1)} %act.1, bf16[512,1024]{1,0:T(8,128)(2,1)} %q_in.1, bf16[512,1024]{1,0:T(8,128)(2,1)} %k_in.1, bf16[512,1024]{1,0:T(8,128)(2,1)} %v_in.1, bf16[512,1024]{1,0:T(8,128)(2,1)} %g_in.1, f32[1,1024]{1,0:T(1,128)} %bitcast.1), custom_call_target="tpu_custom_call" | custom-call | flops 8858370048 | bytes 17825792 | tf_op jit(solution)/shard_map/pallas_call | solution.py:493
  164.3 0.0 copy-start.1
  164.3 0.0 copy-start
  164.4 2.4 %copy.12 = bf16[512,1024]{1,0:T(8,128)(2,1)} copy(bf16[512,1024]{1,0:T(8,128)(2,1)} %get-tuple-element.6) | data formatting | bytes 2097152
  166.8 0.0 copy-done.1
  166.8 1.0 copy.13
  167.7 0.0 copy-done
  167.7 1.3 copy.14
Async XLA Ops:
  164.3 2.4 %copy-start.1 = (bf16[512,1024]{1,0:T(8,128)(2,1)S(1)}, bf16[512,1024]{1,0:T(8,128)(2,1)}, u32[]{:S(2)}) copy-start(bf16[512,1024]{1,0:T(8,128)(2,1)} %get-tuple-element.7) | copy-start | bytes 3145732
  164.3 3.4 %copy-start = (f32[512,1024]{1,0:T(8,128)S(1)}, f32[512,1024]{1,0:T(8,128)}, u32[]{:S(2)}) copy-start(f32[512,1024]{1,0:T(8,128)} %get-tuple-element.8) | copy-start | bytes 6291460

commit v3 on v1

--- a/solution.py
+++ b/solution.py
@@ -50,6 +50,8 @@
     y = me % 2
     pair = me + 1 - 2 * y
     half = rows // 2
+    near_left = z < half
+    near_right = z >= half
 
     def load(i, src, dst):
         return pltpu.make_async_copy(src, dst, in_sem.at[i])
@@ -153,6 +155,10 @@
     ends = has_left.astype(jnp.int32) + has_right.astype(jnp.int32)
     pl.semaphore_wait(barrier, 2 + ends)
 
+    @pl.when(near_right)
+    def _():
+        loop(half, lambda j: send_act(j).start())
+
     loads[0].wait()
     loads[1].wait()
 
@@ -163,7 +169,6 @@
         kv_pair_copy(c).start()
     loop(chunks, summaries)
 
-    loop(half, lambda j: send_act(j).start())
     loop(rows, lambda b: own_act(b).start())
 
     @pl.when(jnp.logical_not(has_left))
@@ -192,6 +197,10 @@
 
     def forward(c):
         kv_pair_copy(c).wait()
+
+        @pl.when(near_left & (c == chunks - 1))
+        def _():
+            loop(half, lambda j: send_act(j).start())
 
         @pl.when(has_left)
         def _():
@@ -224,8 +233,26 @@
         gl_pair_copy(c).start()
     loop(chunks, forward)
 
-    loop(half, lambda j: send_act(j).wait())
-    share_act().start()
+    def carry_grads(c):
+        gl_pair_copy(c).wait()
+
+        @pl.when(has_right)
+        def _():
+            gl_chain(c).wait_recv()
+
+        def one(h, cols):
+            carry = gl_recv[h].astype(F32)
+            other = gl_pair[h].astype(F32)
+            gl_send[h] = (carry + other + gl_mine[h].astype(F32)).astype(BF16)
+        each_head(c, one)
+
+        @pl.when(has_left)
+        def _():
+            gl_chain(c).start()
+
+    @pl.when(jnp.logical_not(has_right))
+    def _():
+        loop(chunks, carry_grads)
 
     def inside(c):
         def one(h, cols):
@@ -242,21 +269,9 @@
     qg_copy.start()
 
     def backward(c):
-        gl_pair_copy(c).wait()
-
         @pl.when(has_right)
         def _():
-            gl_chain(c).wait_recv()
-
-        def one(h, cols):
-            carry = gl_recv[h].astype(F32)
-            other = gl_pair[h].astype(F32)
-            gl_send[h] = (carry + other + gl_mine[h].astype(F32)).astype(BF16)
-        each_head(c, one)
-
-        @pl.when(has_left)
-        def _():
-            gl_chain(c).start()
+            carry_grads(c)
 
         def two(h, cols):
             carry = gl_recv[h].astype(F32)
@@ -275,6 +290,8 @@
     kg_copy.start()
 
     loop(rows, lambda b: own_act(b).wait())
+    loop(half, lambda j: send_act(j).wait())
+    share_act().start()
     share_act().wait()
 
     def term(b, c):

time: 160 us -> 143 us (0.89)
  Pallas kernels: 155 us -> 138 us
    pallas_call x1, Pallas kernels: 155 us -> 138 us  [per_device(): pl.pallas_call(functools.partial(kernel, n, chunks), out_shape=(jax.Shape...]
where the time goes in v3:
time: 143 us
  Pallas kernels  138 us (97%)
  local copies, waits for them, and re-layouts  4.71 us (3%)
    pallas_call x1, Pallas kernels, per_device(): pl.pallas_call(functools.partial(kernel, n, chunks), out_shape=(jax.Shape...  138 us
    unnamed x7, local copies, waits for them, and re-layouts  4.71 us

profile of v3, /device:TPU:0, one launch (start us, length us, event | category | flops | bytes accessed | tf_op | source)
XLA Modules:
  0.0 143.1 jit_solution(1587347662981837320)
XLA Ops:
  0.6 137.7 %shard_map.85 = (bf16[512,1024]{1,0:T(8,128)(2,1)}, bf16[512,1024]{1,0:T(8,128)(2,1)}, f32[512,1024]{1,0:T(8,128)}) custom-call(bf16[512,4096]{1,0:T(8,128)(2,1)} %act.1, bf16[512,1024]{1,0:T(8,128)(2,1)} %q_in.1, bf16[512,1024]{1,0:T(8,128)(2,1)} %k_in.1, bf16[512,1024]{1,0:T(8,128)(2,1)} %v_in.1, bf16[512,1024]{1,0:T(8,128)(2,1)} %g_in.1, f32[1,1024]{1,0:T(1,128)} %bitcast.1), custom_call_target="tpu_custom_call" | custom-call | flops 8858370048 | bytes 17825792 | tf_op jit(solution)/shard_map/pallas_call | solution.py:396
  138.4 0.0 copy-start.1
  138.4 0.0 copy-start
  138.4 2.4 %copy.12 = bf16[512,1024]{1,0:T(8,128)(2,1)} copy(bf16[512,1024]{1,0:T(8,128)(2,1)} %get-tuple-element.6) | data formatting | bytes 2097152
  140.8 0.0 copy-done.1
  140.8 1.0 copy.13
  141.8 0.0 copy-done
  141.8 1.3 copy.14
Async XLA Ops:
  138.4 2.4 %copy-start.1 = (bf16[512,1024]{1,0:T(8,128)(2,1)S(1)}, bf16[512,1024]{1,0:T(8,128)(2,1)}, u32[]{:S(2)}) copy-start(bf16[512,1024]{1,0:T(8,128)(2,1)} %get-tuple-element.7) | copy-start | bytes 3145732
  138.4 3.4 %copy-start = (f32[512,1024]{1,0:T(8,128)S(1)}, f32[512,1024]{1,0:T(8,128)}, u32[]{:S(2)}) copy-start(f32[512,1024]{1,0:T(8,128)} %get-tuple-element.8) | copy-start | bytes 6291460
